TPU v7x, 512 devices: a whole 4x4x16 slice. The times are simulated.
512 devices in a mesh: ctx: 128 (over x, z, core), head: 4 (over y).
Axes of the slice: x: 4, y: 4, z: 16, core: 2. Of those that a mesh axis runs over, the one named last changes fastest.
Arguments:
- queries: bfloat16 [16, 32768, 128], P('head', 'ctx'), may hold values from -6 to 6
- key_vectors: bfloat16 [16, 32768, 128], P('head', 'ctx'), may hold values from -6 to 6
- value_vectors: bfloat16 [16, 32768, 128], P('head', 'ctx'), may hold values from -12 to 12
- norm_gain: float32 [16, 128], P('head'), may hold values from 0.5 to 1.5
- upstream: bfloat16 [16, 32768, 128], P('head', 'ctx'), may hold values from -6 to 6
- cluster_ids: int32 [16, 32768, 1], P('head', 'ctx'), may hold values from 0 to 255; in each aligned block of 256 rows (0 to 255, 256 to 511, ..., all dimensions but the last counted through in order) at most 2 rows name the same one
- positions: int32 [32768], P('ctx'), may hold values from 0 to 32767, each once
Outputs:
- normed_out: bfloat16 [16, 32768, 128], P('head', 'ctx')
- grad_queries: bfloat16 [16, 32768, 128], P('head', 'ctx')
- grad_keys: bfloat16 [16, 32768, 128], P('head', 'ctx')
- grad_values: bfloat16 [16, 32768, 128], P('head', 'ctx')
- centroids: float32 [256, 16, 128], P('ctx', 'head')
Inputs may be any that keep to these rules, and one draw needn't show every extreme that they name: `cluster_ids`: within one head, the 256 tokens of one index of ctx name one cluster at most 2 times. `positions`: every position appears once.
All inputs are finite; a program needn't handle non-finite values.
Results may differ from a plain program's by a relative error of at most 0.02.
Values may be sent and summed in bfloat16 or wider, within the bound.
No kernel may reach another device: no remote copies, remote signals or barrier semaphores. Data moves between devices by JAX's collectives and lax.ppermute only.
A program may use at most 64 MiB of HBM per device.

v0:
```python
import jax
import jax.numpy as jnp
from jax import lax
from jax.sharding import PartitionSpec as P

CLUSTERS = 256
SEND_CAP = 2


def rank_within(member):
    tok_count = member.shape[1]
    matches = member[:, :, None] == member[:, None, :]
    earlier = lax.broadcasted_iota(jnp.int32, (tok_count, tok_count), 0) > lax.broadcasted_iota(
        jnp.int32, (tok_count, tok_count), 1
    )
    return jnp.sum(jnp.logical_and(matches, earlier[None]), axis=2, dtype=jnp.int32)


def to_slots(source, target, filler):

    def place_one(target_row, source_row):
        shape_full = (CLUSTERS * SEND_CAP,) + source_row.shape[1:]
        return jnp.full(shape_full, filler, source_row.dtype).at[target_row].set(source_row)

    placed = jax.vmap(place_one)(target, source)
    return placed.reshape((placed.shape[0], CLUSTERS, SEND_CAP) + source.shape[2:])


def from_slots(buffer, target):
    flattened = buffer.reshape((buffer.shape[0], CLUSTERS * SEND_CAP, buffer.shape[3]))
    return jnp.take_along_axis(flattened, target[:, :, None], axis=1)


def softmax_weights(query_block, key_block, slot_pos, factor):
    scores = (
        jnp.einsum("crd,cjd->crj", query_block, key_block, preferred_element_type=jnp.float32)
        * factor
    )
    allowed = jnp.logical_and(
        slot_pos[:, None, :] >= 0, slot_pos[:, None, :] <= slot_pos[:, :, None]
    )
    scores = jnp.where(allowed, scores, -1e30)
    highest = jnp.max(scores, axis=2, keepdims=True)
    exponent = jnp.exp(scores - highest)
    return exponent / jnp.sum(exponent, axis=2, keepdims=True)


def attend(query_block, key_block, value_block, slot_pos, factor):
    weights = softmax_weights(query_block, key_block, slot_pos, factor)
    rounded = weights.astype(jnp.bfloat16)
    return jnp.einsum(
        "crj,cjd->crd", rounded, value_block, preferred_element_type=jnp.float32
    ).astype(jnp.bfloat16)


def attend_back(query_block, key_block, value_block, slot_pos, grad_block, out_block, factor):
    weights = softmax_weights(query_block, key_block, slot_pos, factor)
    rounded = weights.astype(jnp.bfloat16)
    delta_row = jnp.sum(grad_block.astype(jnp.float32) * out_block.astype(jnp.float32), axis=2)
    grad_value = jnp.einsum(
        "crj,crd->cjd", rounded, grad_block, preferred_element_type=jnp.float32
    ).astype(jnp.bfloat16)
    grad_prob = jnp.einsum(
        "crd,cjd->crj", grad_block, value_block, preferred_element_type=jnp.float32
    )
    grad_score = (factor * weights * (grad_prob - delta_row[:, :, None])).astype(jnp.bfloat16)
    grad_query = jnp.einsum(
        "crj,cjd->crd", grad_score, key_block, preferred_element_type=jnp.float32
    ).astype(jnp.bfloat16)
    grad_key = jnp.einsum(
        "crj,crd->cjd", grad_score, query_block, preferred_element_type=jnp.float32
    ).astype(jnp.bfloat16)
    return (grad_query, grad_key, grad_value)


def local(queries, key_vectors, value_vectors, norm_gain, upstream, cluster_ids, positions):
    head_dev = queries.shape[0]
    feature = queries.shape[2]
    factor = feature ** (-0.5)
    member = cluster_ids[:, :, 0]
    target = member * SEND_CAP + rank_within(member)
    query_slots = to_slots(queries, target, 0)
    key_slots = to_slots(key_vectors, target, 0)
    value_slots = to_slots(value_vectors, target, 0)
    pos_slots = to_slots(jnp.broadcast_to(positions[None, :], member.shape), target, -1)
    query_own, key_own, value_own = (
        lax.all_to_all(query_slots, "ctx", split_axis=1, concat_axis=2, tiled=True),
        lax.all_to_all(key_slots, "ctx", split_axis=1, concat_axis=2, tiled=True),
        lax.all_to_all(value_slots, "ctx", split_axis=1, concat_axis=2, tiled=True),
    )
    pos_own = lax.all_to_all(pos_slots, "ctx", split_axis=1, concat_axis=2, tiled=True)

    def forward_one(blocks):
        return attend(blocks[0], blocks[1], blocks[2], blocks[3], factor)

    out_own = lax.map(forward_one, (query_own, key_own, value_own, pos_own))
    attn_slots = lax.all_to_all(out_own, "ctx", split_axis=2, concat_axis=1, tiled=True)
    attention = from_slots(attn_slots, target).astype(jnp.float32)
    width_all = head_dev * feature * lax.axis_size("head")
    squares = lax.psum(jnp.sum(attention * attention, axis=(0, 2)), "head")
    inverse = lax.rsqrt(squares / width_all + 1e-06)[None, :, None]
    gain_full = norm_gain[:, None, :]
    normed_out = (attention * inverse * gain_full).astype(jnp.bfloat16)
    scaled_grad = gain_full * upstream.astype(jnp.float32)
    dot_total = lax.psum(jnp.sum(scaled_grad * attention, axis=(0, 2)), "head")
    grad_attention = (
        inverse * scaled_grad
        - attention * inverse * inverse * inverse * dot_total[None, :, None] / width_all
    ).astype(jnp.bfloat16)
    grad_slots = to_slots(grad_attention, target, 0)
    query_again, key_again, value_again, grad_own = (
        lax.all_to_all(query_slots, "ctx", split_axis=1, concat_axis=2, tiled=True),
        lax.all_to_all(key_slots, "ctx", split_axis=1, concat_axis=2, tiled=True),
        lax.all_to_all(value_slots, "ctx", split_axis=1, concat_axis=2, tiled=True),
        lax.all_to_all(grad_slots, "ctx", split_axis=1, concat_axis=2, tiled=True),
    )
    pos_again = lax.all_to_all(pos_slots, "ctx", split_axis=1, concat_axis=2, tiled=True)
    out_again = lax.map(forward_one, (query_again, key_again, value_again, pos_again))
    inputs_back = (query_again, key_again, value_again, pos_again, grad_own, out_again)

    def backward_one(blocks):
        return attend_back(blocks[0], blocks[1], blocks[2], blocks[3], blocks[4], blocks[5], factor)

    grad_query_own, grad_key_own, grad_value_own = lax.map(backward_one, inputs_back)
    back_query, back_key, back_value = (
        lax.all_to_all(grad_query_own, "ctx", split_axis=2, concat_axis=1, tiled=True),
        lax.all_to_all(grad_key_own, "ctx", split_axis=2, concat_axis=1, tiled=True),
        lax.all_to_all(grad_value_own, "ctx", split_axis=2, concat_axis=1, tiled=True),
    )
    grad_queries = from_slots(back_query, target)
    grad_keys = from_slots(back_key, target)
    grad_values = from_slots(back_value, target)
    labels = lax.broadcasted_iota(
        jnp.int32, (1, 1, lax.axis_size("ctx") * (CLUSTERS // lax.axis_size("ctx"))), 2
    )
    onehot = (member[:, :, None] == labels).astype(jnp.bfloat16)
    cluster_sums = lax.psum_scatter(
        jnp.einsum("htc,htd->chd", onehot, key_vectors, preferred_element_type=jnp.float32),
        "ctx",
        scatter_dimension=0,
        tiled=True,
    )
    centroids = cluster_sums * lax.rsqrt(
        jnp.mean(cluster_sums * cluster_sums, axis=2, keepdims=True) + 1e-06
    )
    return (normed_out, grad_queries, grad_keys, grad_values, centroids)


def solution(mesh):
    in_specs = (
        P("head", "ctx", None),
        P("head", "ctx", None),
        P("head", "ctx", None),
        P("head", None),
        P("head", "ctx", None),
        P("head", "ctx", None),
        P("ctx"),
    )
    out_specs = (
        P("head", "ctx", None),
        P("head", "ctx", None),
        P("head", "ctx", None),
        P("head", "ctx", None),
        P("ctx", "head", None),
    )
    return jax.shard_map(local, mesh=mesh, in_specs=in_specs, out_specs=out_specs, check_vma=False)
```

profile of v0, /device:TPU:1, one launch (start us, length us, event | category | flops | bytes accessed | tf_op | source)
XLA Modules:
  0.0 765.1 jit_solution(15632500231593127204)
XLA Ops:
  10.2 4.3 scatter_custom_fusion
  15.0 2.3 copy.55
  17.3 20.4 %all-to-all-start = ((s32[4,256,2]{0,2,1:T(2,128)}), s32[4,256,2]{0,2,1:T(2,128)S(1)}, u32[]{:S(2)}, u32[]{:S(2)}) async-start(s32[4,256,2]{0,2,1:T(2,128)} %copy.55), calls=%async_computation | async-start | bytes 524288 | tf_op jit(solution)/shard_map/all_to_all | solution.py:91
  37.7 3.7 scatter_custom_fusion.3
  42.6 17.6 %all-to-all-done = s32[4,256,2]{0,2,1:T(2,128)S(1)} async-done(((s32[4,256,2]{0,2,1:T(2,128)}), s32[4,256,2]{0,2,1:T(2,128)S(1)}, u32[]{:S(2)}, u32[]{:S(2)}) %all-to-all-start) | async-done | bytes 8224 | tf_op jit(solution)/shard_map/all_to_all | solution.py:91
  60.2 7.3 all-to-all-start.3
  67.5 3.3 scatter_custom_fusion.2
  72.0 28.8 %all-to-all-done.3 = bf16[4,256,2,128]{3,2,0,1:T(2,128)(2,1)S(1)} async-done(((bf16[4,256,2,128]{3,2,0,1:T(2,128)(2,1)}), bf16[4,256,2,128]{3,2,0,1:T(2,128)(2,1)S(1)}, u32[]{:S(2)}, u32[]{:S(2)}) %all-to-all-start.3) | async-done | bytes 524320 | tf_op jit(solution)/shard_map/all_to_all | solution.py:89
  100.9 7.2 all-to-all-start.2
  108.0 3.7 scatter_custom_fusion.1
  112.9 28.3 %all-to-all-done.2 = bf16[4,256,2,128]{3,2,0,1:T(2,128)(2,1)S(1)} async-done(((bf16[4,256,2,128]{3,2,0,1:T(2,128)(2,1)}), bf16[4,256,2,128]{3,2,0,1:T(2,128)(2,1)S(1)}, u32[]{:S(2)}, u32[]{:S(2)}) %all-to-all-start.2) | async-done | bytes 524320 | tf_op jit(solution)/shard_map/all_to_all | solution.py:88
  141.2 7.2 all-to-all-start.1
  150.0 31.6 %all-to-all-done.1 = bf16[4,256,2,128]{3,2,0,1:T(2,128)(2,1)S(1)} async-done(((bf16[4,256,2,128]{3,2,0,1:T(2,128)(2,1)}), bf16[4,256,2,128]{3,2,0,1:T(2,128)(2,1)S(1)}, u32[]{:S(2)}, u32[]{:S(2)}) %all-to-all-start.1) | async-done | bytes 524320 | tf_op jit(solution)/shard_map/all_to_all | solution.py:87
  182.2 4.2 while.28
  187.7 7.2 all-to-all-start.4
  194.9 33.2 %all-to-all-done.4 = bf16[4,2,256,128]{3,1,0,2:T(2,128)(2,1)S(1)} async-done(((bf16[4,2,256,128]{3,1,0,2:T(2,128)(2,1)}), bf16[4,2,256,128]{3,1,0,2:T(2,128)(2,1)S(1)}, u32[]{:S(2)}, u32[]{:S(2)}) %all-to-all-start.4) | async-done | bytes 524320 | tf_op jit(solution)/shard_map/all_to_all | solution.py:97
  228.7 5.8 gather_fusion
  235.5 8.9 %all-reduce.1 = (f32[256]{0:T(256)S(1)}, f32[256]{0:T(256)S(1)}) all-reduce(f32[256]{0:T(256)S(1)} %get-tuple-element.172, f32[256]{0:T(256)S(1)} %get-tuple-element.171), channel_id=1, replica_groups=mesh['ctx'=128,'head'=4] {'head'}, use_global_device_ids=true, to_apply=%region_10.12 | all-reduce | flops 512 | bytes 4096 | tf_op jit(solution)/shard_map/psum | solution.py:100
  245.4 3.3 scatter_custom_fusion.4
  250.0 9.2 %all-to-all-start.5 = ((bf16[4,256,2,128]{3,2,0,1:T(2,128)(2,1)}), bf16[4,256,2,128]{3,2,0,1:T(2,128)(2,1)S(1)}, u32[]{:S(2)}, u32[]{:S(2)}) async-start(bf16[4,256,2,128]{3,2,0,1:T(2,128)(2,1)} %copy.70), calls=%async_computation.5 | async-start | bytes 1048576 | tf_op jit(solution)/shard_map/all_to_all | solution.py:115
  259.2 33.2 %all-to-all-done.5 = bf16[4,256,2,128]{3,2,0,1:T(2,128)(2,1)S(1)} async-done(((bf16[4,256,2,128]{3,2,0,1:T(2,128)(2,1)}), bf16[4,256,2,128]{3,2,0,1:T(2,128)(2,1)S(1)}, u32[]{:S(2)}, u32[]{:S(2)}) %all-to-all-start.5) | async-done | bytes 524320 | tf_op jit(solution)/shard_map/all_to_all | solution.py:115
  293.0 21.2 %while.29 = (s32[]{:T(128)}, bf16[4,2,256,128]{3,1,0,2:T(2,128)(2,1)}, bf16[4,2,256,128]{3,1,0,2:T(2,128)(2,1)}, bf16[4,2,256,128]{3,1,0,2:T(2,128)(2,1)S(1)}, s...) while((s32[]{:T(128)}, ...), condition=%wide.region_18.20_spmd, body=%wide.region_14.19_spmd.sunk | while | flops 169935104 | bytes 6837933 | solution.py:124
  299.6 1.3 fusion.166
  304.9 1.3 fusion.166
  314.2 40.3 %all_to_all.170 = bf16[4,2,256,128]{3,1,0,2:T(2,128)(2,1)S(1)} all-to-all(bf16[4,2,256,128]{3,1,0,2:T(2,128)(2,1)S(1)} %get-tuple-element.107), channel_id=1, replica_groups=mesh['ctx'=128,'head'=4] {'ctx'}, dimensions={2} | all-to-all | bytes 1048576 | tf_op jit(solution)/shard_map/all_to_all | solution.py:128
  354.5 40.2 %all_to_all.171 = bf16[4,2,256,128]{3,1,0,2:T(2,128)(2,1)S(1)} all-to-all(bf16[4,2,256,128]{3,1,0,2:T(2,128)(2,1)S(1)} %copy-done.2), channel_id=1, replica_groups=mesh['ctx'=128,'head'=4] {'ctx'}, dimensions={2} | all-to-all | bytes 1048576 | tf_op jit(solution)/shard_map/all_to_all | solution.py:126
  394.6 7.2 all-to-all-start.7
  405.3 330.4 %all-reduce.4.cloned.1.call-done = f32[256,4,128]{2,1,0:T(4,128)} async-done(((f32[256,4,128]{2,1,0:T(4,128)}), f32[256,4,128]{2,1,0:T(4,128)}) %all-reduce.4.cloned.1.call-update) | async-done | bytes 524304
  736.4 1.4 dynamic-slice_multiply_fusion
  738.3 5.8 gather_fusion.3
  744.7 5.8 gather_fusion.1
  751.1 5.8 gather_fusion.2
  (120 shorter events, 43.6 us)
Async XLA Ops:
  7.2 0.7 copy-start
  7.9 0.7 copy-start.4
  8.8 0.7 copy-start.6
  9.5 0.7 copy-start.7
  17.3 42.9 %all-to-all-start = ((s32[4,256,2]{0,2,1:T(2,128)}), s32[4,256,2]{0,2,1:T(2,128)S(1)}, u32[]{:S(2)}, u32[]{:S(2)}) async-start(s32[4,256,2]{0,2,1:T(2,128)} %copy.55), calls=%async_computation | async-start | bytes 524288 | tf_op jit(solution)/shard_map/all_to_all | solution.py:91
  42.6 24.9 %copy-start.3 = (bf16[4,256,128]{2,1,0:T(8,128)(2,1)S(1)}, bf16[4,256,128]{2,1,0:T(8,128)(2,1)}, u32[]{:S(2)}) copy-start(bf16[4,256,128]{2,1,0:T(8,128)(2,1)} %param.14) | copy-start | bytes 786436
  60.2 40.6 %all-to-all-start.3 = ((bf16[4,256,2,128]{3,2,0,1:T(2,128)(2,1)}), bf16[4,256,2,128]{3,2,0,1:T(2,128)(2,1)S(1)}, u32[]{:S(2)}, u32[]{:S(2)}) async-start(bf16[4,256,2,128]{3,2,0,1:T(2,128)(2,1)} %copy.64), calls=%async_computation.3 | async-start | bytes 1048576 | tf_op jit(solution)/shard_map/all_to_all | solution.py:89
  100.9 40.4 %all-to-all-start.2 = ((bf16[4,256,2,128]{3,2,0,1:T(2,128)(2,1)}), bf16[4,256,2,128]{3,2,0,1:T(2,128)(2,1)S(1)}, u32[]{:S(2)}, u32[]{:S(2)}) async-start(bf16[4,256,2,128]{3,2,0,1:T(2,128)(2,1)} %copy.61), calls=%async_computation.2 | async-start | bytes 1048576 | tf_op jit(solution)/shard_map/all_to_all | solution.py:88
  141.2 40.4 %all-to-all-start.1 = ((bf16[4,256,2,128]{3,2,0,1:T(2,128)(2,1)}), bf16[4,256,2,128]{3,2,0,1:T(2,128)(2,1)S(1)}, u32[]{:S(2)}, u32[]{:S(2)}) async-start(bf16[4,256,2,128]{3,2,0,1:T(2,128)(2,1)} %copy.58), calls=%async_computation.1 | async-start | bytes 1048576 | tf_op jit(solution)/shard_map/all_to_all | solution.py:87
  187.7 40.4 %all-to-all-start.4 = ((bf16[4,2,256,128]{3,1,0,2:T(2,128)(2,1)}), bf16[4,2,256,128]{3,1,0,2:T(2,128)(2,1)S(1)}, u32[]{:S(2)}, u32[]{:S(2)}) async-start(bf16[4,2,256,128]{3,1,0,2:T(2,128)(2,1)} %copy.68), calls=%async_computation.4 | async-start | bytes 1048576 | tf_op jit(solution)/shard_map/all_to_all | solution.py:97
  228.7 5.9 copy-start.1
  234.5 0.7 copy-start.5
  250.0 42.4 %all-to-all-start.5 = ((bf16[4,256,2,128]{3,2,0,1:T(2,128)(2,1)}), bf16[4,256,2,128]{3,2,0,1:T(2,128)(2,1)S(1)}, u32[]{:S(2)}, u32[]{:S(2)}) async-start(bf16[4,256,2,128]{3,2,0,1:T(2,128)(2,1)} %copy.70), calls=%async_computation.5 | async-start | bytes 1048576 | tf_op jit(solution)/shard_map/all_to_all | solution.py:115
  294.3 1.3 copy-start.8
  299.6 1.3 copy-start.8
  304.9 1.3 copy-start.8
  310.2 1.3 copy-start.8
  314.2 40.3 %copy-start.2 = (bf16[4,2,256,128]{3,1,0,2:T(2,128)(2,1)S(1)}, bf16[4,2,256,128]{3,1,0,2:T(2,128)(2,1)}, u32[]{:S(2)}) copy-start(bf16[4,2,256,128]{3,1,0,2:T(2,128)(2,1)} %get-tuple-element.105) | copy-start | bytes 1572868
  394.6 355.9 %all-to-all-start.7 = ((bf16[4,2,256,128]{3,1,0,2:T(2,128)(2,1)}), bf16[4,2,256,128]{3,1,0,2:T(2,128)(2,1)S(1)}, u32[]{:S(2)}, u32[]{:S(2)}) async-start(bf16[4,2,256,128]{3,1,0,2:T(2,128)(2,1)} %get-tuple-element.106), calls=%async_computation.7 | async-start | bytes 1048576 | tf_op jit(solution)/shard_map/all_to_all | solution.py:127
  401.8 333.8 %all-reduce.4.cloned.1.call-start = ((), (), s32[]{:S(2)}) async-start(), calls=%async_computation.9 | async-start | bytes 1048576
Sparse Core Ops, SparseCore 0:
  406.1 329.4 all-reduce.3
where the time goes:
time: 774 us; the launch traced here: 765 us
  waiting for transfers between devices  503 us (65%)
  blocking collectives  89.3 us (12%)
  local copies, waits for them, and re-layouts  68.4 us (9%)
  starting transfers between devices  65.5 us (8%)
  matrix products  17.3 us (2%)
  between operations  15.3 us (2%)
    unnamed x2, waiting for transfers between devices  330 us
    all_to_all x1, blocking collectives, local(): lax.all_to_all(grad_value_own, 'ctx', split_axis=2, concat_axis=1, tiled=...  40.3 us
    all_to_all x1, blocking collectives, local(): lax.all_to_all(grad_query_own, 'ctx', split_axis=2, concat_axis=1, tiled=...  40.2 us
    all_to_all x1, waiting for transfers between devices, local(): lax.all_to_all(grad_slots, 'ctx', split_axis=1, concat_axis=2, tiled=True)  33.2 us
    all_to_all x1, waiting for transfers between devices, local(): lax.all_to_all(out_own, 'ctx', split_axis=2, concat_axis=1, tiled=True)  33.2 us
    all_to_all x1, waiting for transfers between devices, local(): lax.all_to_all(query_slots, 'ctx', split_axis=1, concat_axis=2, tiled=True)  31.6 us
    all_to_all x1, waiting for transfers between devices, local(): lax.all_to_all(value_slots, 'ctx', split_axis=1, concat_axis=2, tiled=True)  28.8 us
    all_to_all x1, waiting for transfers between devices, local(): lax.all_to_all(key_slots, 'ctx', split_axis=1, concat_axis=2, tiled=True)  28.3 us
  transfers between devices with their start and end apart: 8, of which 7 were waited for; matrix products, arithmetic and copies ran while one was open for 4% of the time, Pallas kernels for 0%

commit v1 on v0

v1 whole, which is shorter than its diff:
```python
import jax
import jax.numpy as jnp
from jax import lax
from jax.sharding import PartitionSpec as P

CLUSTERS = 256
SEND_CAP = 2


def rank_within(member):
    tok_count = member.shape[1]
    matches = member[:, :, None] == member[:, None, :]
    earlier = lax.broadcasted_iota(jnp.int32, (tok_count, tok_count), 0) > lax.broadcasted_iota(
        jnp.int32, (tok_count, tok_count), 1
    )
    return jnp.sum(jnp.logical_and(matches, earlier[None]), axis=2, dtype=jnp.int32)


def weights_of(query_block, key_block, slot_pos, factor):
    scores = (
        jnp.einsum("urd,ujd->urj", query_block, key_block, preferred_element_type=jnp.float32)
        * factor
    )
    allowed = jnp.logical_and(
        slot_pos[:, None, :] >= 0, slot_pos[:, None, :] <= slot_pos[:, :, None]
    )
    scores = jnp.where(allowed, scores, -1e30)
    highest = jnp.max(scores, axis=2, keepdims=True)
    exponent = jnp.exp(scores - highest)
    return exponent / jnp.sum(exponent, axis=2, keepdims=True)


def local(queries, key_vectors, value_vectors, norm_gain, upstream, cluster_ids, positions):
    heads, tokens, feature = queries.shape
    n_ctx = lax.axis_size("ctx")
    per_dev = CLUSTERS // n_ctx
    factor = feature ** (-0.5)
    member = cluster_ids[:, :, 0]
    target = member * SEND_CAP + rank_within(member)
    slots = CLUSTERS * SEND_CAP
    mine = slots // n_ctx
    onehot = (
        target[:, None, :] == lax.broadcasted_iota(jnp.int32, (1, slots, 1), 1)
    )
    place = onehot.astype(jnp.bfloat16)

    def to_owner(source):
        placed = jnp.einsum(
            "hst,htd->hsd", place, source, preferred_element_type=jnp.float32
        ).astype(jnp.bfloat16)
        placed = placed.reshape(heads, n_ctx, mine, source.shape[2])
        placed = placed.transpose(1, 0, 2, 3).reshape(n_ctx, heads * mine, source.shape[2])
        return lax.all_to_all(placed, "ctx", 0, 0, tiled=True)

    def from_owner(block):
        back = lax.all_to_all(block, "ctx", 0, 0, tiled=True)
        back = back.reshape(n_ctx, heads, mine, block.shape[2])
        back = back.transpose(1, 0, 2, 3).reshape(heads, slots, block.shape[2])
        return jnp.einsum(
            "hst,hsd->htd", place, back, preferred_element_type=jnp.float32
        ).astype(jnp.bfloat16)

    def units(recv):
        width = recv.shape[2]
        block = recv.reshape(n_ctx, heads * per_dev, SEND_CAP, width).transpose(1, 0, 2, 3)
        return block.reshape(heads * per_dev, n_ctx * SEND_CAP, width)

    def ununits(block):
        width = block.shape[2]
        recv = block.reshape(heads * per_dev, n_ctx, SEND_CAP, width).transpose(1, 0, 2, 3)
        return recv.reshape(n_ctx, heads * mine, width)

    pos_slots = jnp.sum(
        jnp.where(onehot, positions[None, None, :] + 1, 0), axis=2, dtype=jnp.int32
    ) - 1
    pos_slots = pos_slots.reshape(heads, n_ctx, mine).transpose(1, 0, 2).reshape(n_ctx, heads * mine)
    pos_recv = lax.all_to_all(pos_slots, "ctx", 0, 0, tiled=True)
    slot_pos = units(pos_recv[:, :, None])[:, :, 0]
    recv = to_owner(jnp.concatenate([queries, key_vectors, value_vectors], axis=2))
    block = units(recv)
    query_own, key_own, value_own = (
        block[:, :, :feature], block[:, :, feature : 2 * feature], block[:, :, 2 * feature :]
    )
    weights = weights_of(query_own, key_own, slot_pos, factor)
    rounded = weights.astype(jnp.bfloat16)
    out_own = jnp.einsum(
        "urj,ujd->urd", rounded, value_own, preferred_element_type=jnp.float32
    ).astype(jnp.bfloat16)
    attention = from_owner(ununits(out_own)).astype(jnp.float32)
    width_all = heads * feature * lax.axis_size("head")
    gain_full = norm_gain[:, None, :]
    scaled_grad = gain_full * upstream.astype(jnp.float32)
    sums = lax.psum(
        jnp.stack(
            [
                jnp.sum(attention * attention, axis=(0, 2)),
                jnp.sum(scaled_grad * attention, axis=(0, 2)),
            ]
        ),
        "head",
    )
    inverse = lax.rsqrt(sums[0] / width_all + 1e-06)[None, :, None]
    dot_total = sums[1][None, :, None]
    normed_out = (attention * inverse * gain_full).astype(jnp.bfloat16)
    grad_attention = (
        inverse * scaled_grad
        - attention * inverse * inverse * inverse * dot_total / width_all
    ).astype(jnp.bfloat16)
    grad_block = units(to_owner(grad_attention))
    delta_row = jnp.sum(grad_block.astype(jnp.float32) * out_own.astype(jnp.float32), axis=2)
    grad_value = jnp.einsum(
        "urj,urd->ujd", rounded, grad_block, preferred_element_type=jnp.float32
    ).astype(jnp.bfloat16)
    grad_prob = jnp.einsum(
        "urd,ujd->urj", grad_block, value_own, preferred_element_type=jnp.float32
    )
    grad_score = (factor * weights * (grad_prob - delta_row[:, :, None])).astype(jnp.bfloat16)
    grad_query = jnp.einsum(
        "urj,ujd->urd", grad_score, key_own, preferred_element_type=jnp.float32
    ).astype(jnp.bfloat16)
    grad_key = jnp.einsum(
        "urj,urd->ujd", grad_score, query_own, preferred_element_type=jnp.float32
    ).astype(jnp.bfloat16)
    grads = from_owner(ununits(jnp.concatenate([grad_query, grad_key, grad_value], axis=2)))
    cluster_sums = jnp.sum(key_own.astype(jnp.float32), axis=1)
    cluster_sums = cluster_sums.reshape(heads, per_dev, feature).transpose(1, 0, 2)
    centroids = cluster_sums * lax.rsqrt(
        jnp.mean(cluster_sums * cluster_sums, axis=2, keepdims=True) + 1e-06
    )
    return (
        normed_out,
        grads[:, :, :feature],
        grads[:, :, feature : 2 * feature],
        grads[:, :, 2 * feature :],
        centroids,
    )


def solution(mesh):
    tok = P("head", "ctx", None)
    in_specs = (tok, tok, tok, P("head", None), tok, tok, P("ctx"))
    out_specs = (tok, tok, tok, tok, P("ctx", "head", None))
    return jax.shard_map(local, mesh=mesh, in_specs=in_specs, out_specs=out_specs, check_vma=False)
```

time: 774 us -> 323 us (0.42); the launches traced: 765 us -> 323 us
  waiting for transfers between devices: 503 us -> 194 us
  local copies, waits for them, and re-layouts: 68.4 us -> 18.7 us
  blocking collectives: 89.3 us -> 51 us
  starting transfers between devices: 65.5 us -> 43 us
  between operations: 15.3 us -> 1.01 us
    unnamed x2 -> x0, waiting for transfers between devices: 330 us -> none
    all_to_all x2 -> x1, blocking collectives: 80.4 us -> 42.3 us  [to_owner(): return lax.all_to_all(placed, 'ctx', 0, 0, tiled=True)]
    gather x4 -> x0, local copies, waits for them, and re-layouts: 23.3 us -> none  [from_slots(): return jnp.take_along_axis(flattened, target[:, :, None], axis=1)]
    all_to_all x7 -> x4, starting transfers between devices: 65.5 us -> 43 us  [the longest x1 20.4 us: local(): pos_recv = lax.all_to_all(pos_slots, 'ctx', 0, 0, tiled=True)]
    all_to_all x7 -> x4, waiting for transfers between devices: 173 us -> 194 us  [the longest x2 107 us: from_owner(): back = lax.all_to_all(block, 'ctx', 0, 0, tiled=True)]
    unnamed x28 -> x16, local copies, waits for them, and re-layouts: 22.9 us -> 2.31 us
  transfers between devices with their start and end apart: 8 -> 4, of which waited for: 7 -> 4; matrix products, arithmetic and copies ran while one was open for 4% -> 3% of each run, Pallas kernels for 0% -> 0%
where the time goes in v1:
time: 323 us
  waiting for transfers between devices  194 us (60%)
  blocking collectives  51 us (16%)
  starting transfers between devices  43 us (13%)
  local copies, waits for them, and re-layouts  18.7 us (6%)
  matrix products  11.4 us (4%)
  other arithmetic  4.03 us (1%)
    all_to_all x2, waiting for transfers between devices, from_owner(): back = lax.all_to_all(block, 'ctx', 0, 0, tiled=True)  107 us
    all_to_all x1, waiting for transfers between devices, to_owner(): return lax.all_to_all(placed, 'ctx', 0, 0, tiled=True)  76.5 us
    all_to_all x1, blocking collectives, to_owner(): return lax.all_to_all(placed, 'ctx', 0, 0, tiled=True)  42.3 us
    all_to_all x1, starting transfers between devices, local(): pos_recv = lax.all_to_all(pos_slots, 'ctx', 0, 0, tiled=True)  20.4 us
    all_to_all x2, starting transfers between devices, from_owner(): back = lax.all_to_all(block, 'ctx', 0, 0, tiled=True)  16 us
    all_to_all x1, waiting for transfers between devices, local(): pos_recv = lax.all_to_all(pos_slots, 'ctx', 0, 0, tiled=True)  10.1 us
    psum x1, blocking collectives, local(): lax.psum(jnp.stack([jnp.sum(attention * attention, axis=(0, 2)), jnp.sum(...  8.73 us
    all_to_all x1, starting transfers between devices, to_owner(): return lax.all_to_all(placed, 'ctx', 0, 0, tiled=True)  6.58 us
  transfers between devices with their start and end apart: 4, of which 4 were waited for; matrix products, arithmetic and copies ran while one was open for 3% of the time, Pallas kernels for 0%

profile of v1, /device:TPU:1, one launch (start us, length us, event | category | flops | bytes accessed | tf_op | source)
XLA Modules:
  0.0 322.7 jit_solution(3992617199061359926)
XLA Ops:
  0.7 0.7 copy.153
  1.8 0.7 multiply_add_fusion
  2.4 0.7 broadcast_add_fusion.1
  3.8 0.7 copy.97
  4.6 20.4 %all-to-all-start = ((s32[128,1,16]{2,1,0:T(1,128)}), s32[128,1,16]{2,1,0:T(1,128)S(1)}, u32[]{:S(2)}, u32[]{:S(2)}) async-start(s32[128,1,16]{2,1,0:T(1,128)} %copy.97), calls=%async_computation | async-start | bytes 131072 | tf_op jit(solution)/shard_map/all_to_all | solution.py:77
  25.0 2.1 fusion.5
  27.8 2.1 copy.105
  29.8 10.1 %all-to-all-done = s32[128,1,16]{2,1,0:T(1,128)S(1)} async-done(((s32[128,1,16]{2,1,0:T(1,128)}), s32[128,1,16]{2,1,0:T(1,128)S(1)}, u32[]{:S(2)}, u32[]{:S(2)}) %all-to-all-start) | async-done | bytes 8224 | tf_op jit(solution)/shard_map/all_to_all | solution.py:77
  39.9 6.6 %all-to-all-start.1 = ((bf16[128,16,384]{2,1,0:T(8,128)(2,1)}), bf16[128,16,384]{2,1,0:T(8,128)(2,1)S(1)}, u32[]{:S(2)}, u32[]{:S(2)}) async-start(bf16[128,16,384]{2,1,0:T(8,128)(2,1)} %copy.105), calls=%async_computation.1 | async-start | bytes 3145728 | tf_op jit(solution)/shard_map/all_to_all | solution.py:53
  46.9 76.5 %all-to-all-done.1 = bf16[128,16,384]{2,1,0:T(8,128)(2,1)S(1)} async-done(((bf16[128,16,384]{2,1,0:T(8,128)(2,1)}), bf16[128,16,384]{2,1,0:T(8,128)(2,1)S(1)}, u32[]{:S(2)}, u32[]{:S(2)}) %all-to-all-start.1) | async-done | bytes 1572896 | tf_op jit(solution)/shard_map/all_to_all | solution.py:53
  123.8 1.6 copy.107
  125.4 0.6 reshape.125
  126.1 2.8 fusion.49
  128.9 2.1 convolution_convert_fusion.4
  131.1 1.2 copy.110
  132.3 8.7 %all-to-all-start.2 = ((bf16[128,16,128]{2,1,0:T(8,128)(2,1)}), bf16[128,16,128]{2,1,0:T(8,128)(2,1)S(1)}, u32[]{:S(2)}, u32[]{:S(2)}) async-start(bf16[128,16,128]{2,1,0:T(8,128)(2,1)} %copy.110), calls=%async_computation.2 | async-start | bytes 1048576 | tf_op jit(solution)/shard_map/all_to_all | solution.py:56
  141.2 33.0 %all-to-all-done.2 = bf16[128,16,128]{2,1,0:T(8,128)(2,1)S(1)} async-done(((bf16[128,16,128]{2,1,0:T(8,128)(2,1)}), bf16[128,16,128]{2,1,0:T(8,128)(2,1)S(1)}, u32[]{:S(2)}, u32[]{:S(2)}) %all-to-all-start.2) | async-done | bytes 524320 | tf_op jit(solution)/shard_map/all_to_all | solution.py:56
  174.8 1.0 multiply_reduce_fusion.2
  175.8 8.7 %psum.7 = f32[2,256]{1,0:T(2,128)S(1)} all-reduce(f32[2,256]{1,0:T(2,128)S(1)} %pad_maximum_fusion.1), channel_id=1, replica_groups=mesh['ctx'=128,'head'=4] {'head'}, use_global_device_ids=true, to_apply=%region_6.7 | all-reduce | flops 512 | bytes 4096 | tf_op jit(solution)/shard_map/psum | solution.py:93
  184.5 0.8 convolution_convert_fusion
  185.8 42.3 %all_to_all.29 = bf16[128,16,128]{2,1,0:T(8,128)(2,1)S(1)} all-to-all(bf16[128,16,128]{2,1,0:T(8,128)(2,1)S(1)} %copy.119), channel_id=1, replica_groups=mesh['ctx'=128,'head'=4] {'ctx'}, dimensions={0} | all-to-all | bytes 1048576 | tf_op jit(solution)/shard_map/all_to_all | solution.py:53
  228.3 0.5 copy.121
  231.2 1.3 copy.129
  232.9 2.1 copy.131
  235.0 7.3 %all-to-all-start.4 = ((bf16[128,16,384]{2,1,0:T(8,128)(2,1)}), bf16[128,16,384]{2,1,0:T(8,128)(2,1)S(1)}, u32[]{:S(2)}, u32[]{:S(2)}) async-start(bf16[128,16,384]{2,1,0:T(8,128)(2,1)} %copy.131), calls=%async_computation.4 | async-start | bytes 3145728 | tf_op jit(solution)/shard_map/all_to_all | solution.py:56
  242.3 1.1 convert_reduce_fusion
  243.6 0.6 copy.135
  244.3 0.8 copy.134
  245.1 73.9 %all-to-all-done.4 = bf16[128,16,384]{2,1,0:T(8,128)(2,1)S(1)} async-done(((bf16[128,16,384]{2,1,0:T(8,128)(2,1)}), bf16[128,16,384]{2,1,0:T(8,128)(2,1)S(1)}, u32[]{:S(2)}, u32[]{:S(2)}) %all-to-all-start.4) | async-done | bytes 1572896 | tf_op jit(solution)/shard_map/all_to_all | solution.py:56
  319.4 1.2 copy.133
  321.0 0.8 fusion.6
  321.8 0.9 fusion.47
  (48 shorter events, 7.7 us)
Async XLA Ops:
  4.6 35.4 %all-to-all-start = ((s32[128,1,16]{2,1,0:T(1,128)}), s32[128,1,16]{2,1,0:T(1,128)S(1)}, u32[]{:S(2)}, u32[]{:S(2)}) async-start(s32[128,1,16]{2,1,0:T(1,128)} %copy.97), calls=%async_computation | async-start | bytes 131072 | tf_op jit(solution)/shard_map/all_to_all | solution.py:77
  39.9 83.5 %all-to-all-start.1 = ((bf16[128,16,384]{2,1,0:T(8,128)(2,1)}), bf16[128,16,384]{2,1,0:T(8,128)(2,1)S(1)}, u32[]{:S(2)}, u32[]{:S(2)}) async-start(bf16[128,16,384]{2,1,0:T(8,128)(2,1)} %copy.105), calls=%async_computation.1 | async-start | bytes 3145728 | tf_op jit(solution)/shard_map/all_to_all | solution.py:53
  126.1 104.6 %copy-start = (bf16[8,256,384]{2,1,0:T(8,128)(2,1)}, bf16[8,256,384]{2,1,0:T(8,128)(2,1)S(1)}, u32[]{:S(2)}) copy-start(bf16[8,256,384]{2,1,0:T(8,128)(2,1)S(1)} %reshape.125) | copy-start | bytes 4718596
  131.0 10.0 %copy-start.3 = (bf16[4,256,128]{2,1,0:T(8,128)(2,1)S(1)}, bf16[4,256,128]{2,1,0:T(8,128)(2,1)}, u32[]{:S(2)}) copy-start(bf16[4,256,128]{2,1,0:T(8,128)(2,1)} %param.11) | copy-start | bytes 786436
  132.3 42.5 %copy-start.4 = (f32[4,128]{1,0:T(4,128)S(1)}, f32[4,128]{1,0:T(4,128)}, u32[]{:S(2)}) copy-start(f32[4,128]{1,0:T(4,128)} %param.10) | copy-start | bytes 6148
  132.3 41.9 %all-to-all-start.2 = ((bf16[128,16,128]{2,1,0:T(8,128)(2,1)}), bf16[128,16,128]{2,1,0:T(8,128)(2,1)S(1)}, u32[]{:S(2)}, u32[]{:S(2)}) async-start(bf16[128,16,128]{2,1,0:T(8,128)(2,1)} %copy.110), calls=%async_computation.2 | async-start | bytes 1048576 | tf_op jit(solution)/shard_map/all_to_all | solution.py:56
  175.7 9.6 %copy-start.1 = (f32[4,256,128]{1,2,0:T(8,128)}, f32[4,256,128]{1,2,0:T(8,128)S(1)}, u32[]{:S(2)}) copy-start(f32[4,256,128]{1,2,0:T(8,128)S(1)} %get-tuple-element.34) | copy-start | bytes 1572868
  185.4 43.4 %copy-start.5 = (f32[8,256,256]{1,2,0:T(8,128)S(1)}, f32[8,256,256]{1,2,0:T(8,128)}, u32[]{:S(2)}) copy-start(f32[8,256,256]{1,2,0:T(8,128)} %get-tuple-element.33) | copy-start | bytes 6291460
  235.0 9.2 %copy-start.2 = (f32[4,256,128]{1,2,0:T(8,128)S(1)}, f32[4,256,128]{1,2,0:T(8,128)}, u32[]{:S(2)}) copy-start(f32[4,256,128]{1,2,0:T(8,128)} %copy-done.1) | copy-start | bytes 1572868
  235.0 84.1 %all-to-all-start.4 = ((bf16[128,16,384]{2,1,0:T(8,128)(2,1)}), bf16[128,16,384]{2,1,0:T(8,128)(2,1)S(1)}, u32[]{:S(2)}, u32[]{:S(2)}) async-start(bf16[128,16,384]{2,1,0:T(8,128)(2,1)} %copy.131), calls=%async_computation.4 | async-start | bytes 3145728 | tf_op jit(solution)/shard_map/all_to_all | solution.py:56
